TPU v7x, 32 devices: a whole 2x2x4 slice. The times are simulated.
32 devices in a mesh: groups: 1, date: 32 (over z, y, x, core), tile: 1, pol: 1.
Axes of the slice: x: 2, y: 2, z: 4, core: 2. Of those that a mesh axis runs over, the one named last changes fastest.
Arguments:
- slc: bfloat16 [2, 256, 16, 128], P(None, ('date', 'pol'), ('groups', 'tile')), as said below
- date_group: int32 [32], replicated, may hold values from 0 to 31, each once
- ref_blocks: int32 [16], replicated, may hold values from 0 to 15, each once
- look_offsets: int32 [4], replicated, may hold values from 0 to 3, each once
Outputs:
- coherence: float32 [2, 4, 32, 64, 256], P(None, ('groups', 'tile', 'pol'), 'date')
Inputs may be any that keep to these rules, and one draw needn't show every extreme that they name: `date_group`: a permutation; storage rows s*8 + k hold date date_group[s]*8 + k. `ref_blocks`: a permutation of the date blocks. `look_offsets`: a permutation. `slc`: every pixel's amplitude sqrt(re^2 + im^2) lies between 0.49 and 2.02.
All inputs are finite; a program needn't handle non-finite values.
Results may differ from a plain program's by a relative error of at most 0.0003.
Values may be sent and summed in bfloat16 or wider, within the bound.
A program may use at most 64 MiB of HBM per device.

v0:
```python
import jax
import jax.numpy as jnp
from jax import lax
from jax.sharding import PartitionSpec as P

DATES = 256
REF_BLK = 16
NREF = 4
STRIDE = 4
WIN = 9


def with_halo(cells, sides, width):
    for axis, dim in sides:
        count = lax.axis_size(axis)
        ends = count - 1
        head = lax.slice_in_dim(cells, 0, width, axis=dim)
        tail = lax.slice_in_dim(cells, cells.shape[dim] - width, cells.shape[dim], axis=dim)
        cells = jnp.concatenate(
            [
                lax.ppermute(tail, axis, [(i, (i + 1) % count) for i in range(ends)]),
                cells,
                lax.ppermute(head, axis, [((i + 1) % count, i) for i in range(ends)]),
            ],
            axis=dim,
        )
    return cells


def from_root(value, axis, source):
    kept = jnp.where(lax.axis_index(axis) == source, value, 0).astype(value.dtype)
    return lax.psum(kept, axis)


def box_matrix(look_count, cell_count, grid_offset, cell_shift):
    look_ids = jnp.arange(look_count, dtype=jnp.int32)[:, None]
    cell_ids = jnp.arange(cell_count, dtype=jnp.int32)[None, :]
    distance = jnp.abs(cell_ids - cell_shift - STRIDE * look_ids - grid_offset)
    return (distance <= WIN // 2).astype(jnp.float32)


def windowed(surface, row_box, col_box):
    across = jnp.einsum("...qw,cw->...qc", surface, col_box, precision=lax.Precision.HIGHEST)
    return jnp.einsum("aq,...qc->...ac", row_box, across, precision=lax.Precision.HIGHEST)


def slot_order(date_group, dates_here):
    block_count = date_group.shape[0]
    block_ids = jnp.arange(block_count, dtype=jnp.int32)
    matches = (date_group[None, :] == block_ids[:, None]).astype(jnp.int32)
    inverse = jnp.sum(matches * block_ids[None, :], axis=1)
    date_slots = inverse[:, None] * dates_here + jnp.arange(dates_here, dtype=jnp.int32)[None, :]
    return (inverse, date_slots.reshape(-1))


def pair_terms(real_one, imag_one, real_many, imag_many):
    return jnp.stack(
        [real_one * real_many + imag_one * imag_many, imag_one * real_many - real_one * imag_many]
    )


def body(slc, date_group, ref_blocks, look_offsets):
    dates_here = slc.shape[1]
    row_count = slc.shape[2]
    col_count = slc.shape[3]
    rim_width = WIN // 2
    pol_count = lax.axis_size("pol")
    date_count = lax.axis_size("date")
    look_rows = row_count // STRIDE
    rows_part = look_rows // pol_count
    cols_part = col_count // STRIDE // date_count
    ref_total = NREF * REF_BLK
    inverse, date_slots = slot_order(date_group, dates_here)
    rimmed = with_halo(slc, (("tile", 2),), rim_width)
    span_dates = min(dates_here, REF_BLK)
    row_box = box_matrix(look_rows, row_count + 2 * rim_width, look_offsets[0], rim_width)
    col_box = box_matrix(col_count // STRIDE, col_count, look_offsets[1], 0)
    local_vals = rimmed.astype(jnp.float32)
    local_power = windowed(
        local_vals[0] * local_vals[0] + local_vals[1] * local_vals[1], row_box, col_box
    )
    results = []
    for ref_block in range(NREF):
        portions = []
        for portion_no in range(REF_BLK // span_dates):
            first_date = ref_blocks[ref_block] * REF_BLK + portion_no * span_dates
            holder = inverse[first_date // dates_here]
            portions.append(from_root(rimmed, ("date", "pol"), holder))
        ref_rows = jnp.concatenate(portions, axis=1)
        ref_vals = ref_rows.astype(jnp.float32)
        ref_power = windowed(
            ref_vals[0] * ref_vals[0] + ref_vals[1] * ref_vals[1], row_box, col_box
        )

        def one_date(entries, ref_vals=ref_vals, ref_power=ref_power):
            real_one, imag_one, own_power = entries
            numerator = windowed(
                pair_terms(real_one[None], imag_one[None], ref_vals[0], ref_vals[1]),
                row_box,
                col_box,
            )
            return numerator / jnp.sqrt(own_power[None, None] * ref_power[None])

        results.append(lax.map(one_date, (local_vals[0], local_vals[1], local_power)))
    coherence = jnp.concatenate(results, axis=2)
    arranged = coherence.reshape(
        dates_here, 2, ref_total, pol_count, rows_part, date_count, cols_part
    )
    arranged = jnp.transpose(arranged, (1, 0, 2, 5, 3, 4, 6)).reshape(
        2, dates_here, ref_total, date_count * pol_count, rows_part * cols_part
    )
    arrived = lax.all_to_all(arranged, ("date", "pol"), split_axis=3, concat_axis=1, tiled=True)
    ordered = jnp.take(arrived, date_slots, axis=1).reshape(
        2, DATES, ref_total, rows_part, cols_part
    )
    return jnp.transpose(ordered, (0, 3, 4, 2, 1))


def solution(mesh):
    return jax.shard_map(
        body,
        mesh=mesh,
        in_specs=(P(None, ("date", "pol"), ("groups", "tile"), None), P(), P(), P()),
        out_specs=P(None, ("groups", "tile", "pol"), "date", None, None),
        check_vma=False,
    )
```

profile of v0, /device:TPU:0, one launch (start us, length us, event | category | flops | bytes accessed | tf_op | source)
XLA Modules:
  0.0 306.3 jit_solution(11780476112226263025)
XLA Ops:
  9.5 1.3 fusion.140
  10.9 1.5 fusion.142
  21.3 1.6 broadcast_select_fusion.7
  24.9 134.4 %all-reduce.3.cloned.1.call-done = (bf16[2,8,24,128]{3,2,1,0:T(8,128)(2,1)}, bf16[2,8,24,128]{3,2,1,0:T(8,128)(2,1)}, bf16[2,8,24,128]{3,2,1,0:T(8,128)(2,1)}, b...) async-done(((bf16[2,8,24,128]{3,2,1,0:T(8,128)(2,1)}, ...) | async-done | bytes 786448 | tf_op jit(solution)/shard_map/psum | solution.py:32
  161.5 18.2 %while.46 = (s32[]{:T(128)}, f32[8,2,16,4,32]{4,3,2,1,0:T(4,128)S(1)}, f32[8,24,128]{2,1,0:T(8,128)S(1)}, f32[2,16,24,128]{3,2,1,0:T(8,128)S(1)}, f32[8,24,128]{...) while((s32[]{:T(128)}, ...), condition=%wide.region_12.13_spmd.clone, body=%wide.region_11.12_spmd.clone.sunk | while | flops 39348704 | bytes 1864473 | solution.py:104
  163.9 1.1 fusion.198
  166.2 1.1 fusion.198
  168.5 1.1 fusion.198
  170.8 1.1 fusion.198
  173.0 1.1 fusion.198
  177.6 1.1 fusion.198
  180.9 18.2 %while.47 = (s32[]{:T(128)}, f32[8,2,16,4,32]{4,3,2,1,0:T(4,128)S(1)}, f32[8,24,128]{2,1,0:T(8,128)S(1)}, f32[2,16,24,128]{3,2,1,0:T(8,128)S(1)}, f32[8,24,128]{...) while((s32[]{:T(128)}, ...), condition=%wide.region_16.17_spmd.clone, body=%wide.region_15.16_spmd.clone.sunk | while | flops 39348704 | bytes 1864473 | solution.py:104
  181.1 1.1 fusion.204
  203.0 28.9 %while.44 = (s32[]{:T(128)}, f32[8,2,16,4,32]{4,3,2,1,0:T(4,128)S(1)}, f32[8,24,128]{2,1,0:T(8,128)}, f32[2,16,24,128]{3,2,1,0:T(8,128)S(1)}, f32[8,24,128]{2,1,...) while((s32[]{:T(128)}, ...), condition=%wide.region_4.5_spmd.clone, body=%wide.region_3.4_spmd.clone.sunk | while | flops 39348704 | bytes 1864473 | solution.py:104
  208.1 1.1 fusion.186
  211.7 1.1 fusion.186
  218.9 1.1 fusion.186
  222.5 1.1 fusion.186
  233.7 28.9 %while.45 = (s32[]{:T(128)}, f32[8,2,16,4,32]{4,3,2,1,0:T(4,128)S(1)}, f32[8,24,128]{2,1,0:T(8,128)}, f32[2,16,24,128]{3,2,1,0:T(8,128)S(1)}, f32[8,24,128]{2,1,...) while((s32[]{:T(128)}, ...), condition=%wide.region_8.9_spmd.clone, body=%wide.region_7.8_spmd.clone.sunk | while | flops 39348704 | bytes 1864473 | solution.py:104
  235.2 1.1 fusion.192
  238.8 1.1 fusion.192
  253.2 1.1 fusion.192
  260.4 1.1 fusion.192
  263.4 2.0 copy.16
  265.3 2.8 copy.15
  268.1 3.1 %fusion.143 = f32[32,2,4,8,64]{4,3,2,1,0:T(8,128)} fusion(f32[8,2,16,4,32]{2,0,3,1,4:T(8,128)S(1)} %copy.18, f32[8,2,16,4,32]{2,0,3,1,4:T(8,128)S(1)} %copy.17, f32[8,2,16,4,32]{2,0,3,1,4:T(8,128)S(1)} %copy.16, f32[8,2,16,4,32]{2,0,3,1,4:T(8,128)} %copy.15), kind=kLoop, calls=%fused_computation.208 | loop fusion | flops 393216 | bytes 1048576
  271.2 2.7 reshape.162
  273.9 3.7 %all-to-all-start = ((f32[32,1,4096]{2,1,0:T(1,128)}), f32[32,1,4096]{2,1,0:T(1,128)S(1)}, u32[]{:S(2)}, u32[]{:S(2)}) async-start(f32[32,1,4096]{2,1,0:T(1,128)} %reshape.162), calls=%async_computation | async-start | bytes 1048576 | tf_op jit(solution)/shard_map/all_to_all | solution.py:112
  277.8 15.1 %all-to-all-done = f32[32,1,4096]{2,1,0:T(1,128)S(1)} async-done(((f32[32,1,4096]{2,1,0:T(1,128)}), f32[32,1,4096]{2,1,0:T(1,128)S(1)}, u32[]{:S(2)}, u32[]{:S(2)}) %all-to-all-start) | async-done | bytes 524320 | tf_op jit(solution)/shard_map/all_to_all | solution.py:112
  293.4 1.9 reduce
  296.5 1.4 gather_fusion
  298.2 1.3 copy.21
  (274 shorter events, 93.8 us)
Async XLA Ops:
  6.5 17.3 %copy-start.3 = (bf16[2,8,16,128]{3,2,1,0:T(8,128)(2,1)S(1)}, bf16[2,8,16,128]{3,2,1,0:T(8,128)(2,1)}, u32[]{:S(2)}) copy-start(bf16[2,8,16,128]{3,2,1,0:T(8,128)(2,1)} %param.12) | copy-start | bytes 196612
  6.5 152.7 %all-reduce.3.cloned.1.call-start = ((), (), s32[]{:S(2)}) async-start(), calls=%async_computation.1 | async-start | bytes 1572864 | tf_op jit(solution)/shard_map/psum | solution.py:32
  7.4 13.9 %collective-permute-start = (bf16[2,8,4,128]{3,2,1,0:T(4,128)(2,1)S(1)}, bf16[2,8,4,128]{3,2,1,0:T(4,128)(2,1)S(1)}, u32[]{:S(2)}, u32[]{:S(2)}) collective-permute-start(bf16[2,8,4,128]{3,2,1,0:T(4,128)(2,1)S(1)} %get-tuple-element.456), channel_id=1, source_target_pairs={} | collective-permute-start | bytes 49160 | tf_op jit(solution)/shard_map/ppermute | solution.py:21
  8.0 13.3 %collective-permute-start.1 = (bf16[2,8,4,128]{3,2,1,0:T(4,128)(2,1)S(1)}, bf16[2,8,4,128]{3,2,1,0:T(4,128)(2,1)S(1)}, u32[]{:S(2)}, u32[]{:S(2)}) collective-permute-start(bf16[2,8,4,128]{3,2,1,0:T(4,128)(2,1)S(1)} %get-tuple-element.457), channel_id=1, source_target_pairs={} | collective-permute-start | bytes 49160 | tf_op jit(solution)/shard_map/ppermute | solution.py:23
  13.0 189.7 %copy-start.9 = (pred[4,24,1]{1,0,2:T(4,128)(4,1)}, pred[4,24,1]{1,0,2:T(4,128)(4,1)S(1)}, u32[]{:S(2)}) copy-start(pred[4,24,1]{1,0,2:T(4,128)(4,1)S(1)} %fusion.132) | copy-start | bytes 292
  199.1 0.6 copy-start.2
  199.7 1.9 copy-start.4
  200.7 1.0 copy-start.5
  200.7 1.0 copy-start.6
  200.7 1.0 copy-start.7
  200.7 1.0 copy-start.8
  231.9 0.9 copy-start.1
  262.6 0.8 copy-start
  273.9 19.0 %all-to-all-start = ((f32[32,1,4096]{2,1,0:T(1,128)}), f32[32,1,4096]{2,1,0:T(1,128)S(1)}, u32[]{:S(2)}, u32[]{:S(2)}) async-start(f32[32,1,4096]{2,1,0:T(1,128)} %reshape.162), calls=%async_computation | async-start | bytes 1048576 | tf_op jit(solution)/shard_map/all_to_all | solution.py:112
Sparse Core Ops, SparseCore 0:
  24.8 134.3 all-reduce.2
where the time goes:
time: 309 us; the launch traced here: 306 us
  waiting for transfers between devices  149 us (48%)
  matrix products  73.9 us (24%)
  local copies, waits for them, and re-layouts  42.6 us (14%)
  between operations  21.4 us (7%)
  other arithmetic  12.4 us (4%)
  starting transfers between devices  4.96 us (2%)
    psum x1, waiting for transfers between devices, from_root(): return lax.psum(kept, axis)  134 us
    dot_general x37, matrix products, windowed(): jnp.einsum('...qw,cw->...qc', surface, col_box, precision=lax.Precision.H...  40.6 us
    dot_general x37, matrix products, windowed(): jnp.einsum('aq,...qc->...ac', row_box, across, precision=lax.Precision.HI...  33.3 us
    all_to_all x1, waiting for transfers between devices, body(): lax.all_to_all(arranged, ('date', 'pol'), split_axis=3, concat_axis=1, ti...  15.1 us
    mul x32, local copies, waits for them, and re-layouts, pair_terms(): imag_one * imag_many  11.5 us
    mul x32, local copies, waits for them, and re-layouts, one_date(): return numerator / jnp.sqrt(own_power[None, None] * ref_power[None])  10.9 us
    while x4, local copies, waits for them, and re-layouts, body(): lax.map(one_date, (local_vals[0], local_vals[1], local_power))  6.59 us
  transfers between devices with their start and end apart: 4, of which 2 were waited for; matrix products, arithmetic and copies ran while one was open for 2% of the time, Pallas kernels for 0%

commit v1 on v0

v1 whole, which is shorter than its diff:
```python
import functools

import jax
import jax.numpy as jnp
from jax import lax
from jax.experimental import pallas as pl
from jax.experimental.pallas import tpu as pltpu
from jax.sharding import PartitionSpec as P

REF_BLK = 16
NREF = 4
STRIDE = 4
WIN = 9
RIM = WIN // 2
SPAN = 3


def with_halo(cells, axis, dim, width):
    count = lax.axis_size(axis)
    ends = count - 1
    head = lax.slice_in_dim(cells, 0, width, axis=dim)
    tail = lax.slice_in_dim(cells, cells.shape[dim] - width, cells.shape[dim], axis=dim)
    return jnp.concatenate(
        [
            lax.ppermute(tail, axis, [(i, i + 1) for i in range(ends)]),
            cells,
            lax.ppermute(head, axis, [(i + 1, i) for i in range(ends)]),
        ],
        axis=dim,
    )


def nt_dot(a, b):
    return lax.dot_general(
        a, b, (((1,), (1,)), ((), ())), preferred_element_type=jnp.float32
    )


def iota(shape, dim):
    return lax.broadcasted_iota(jnp.int32, shape, dim)


def pack(x_ref, p, col_blocks):
    _, _, days, rows, cols = x_ref.shape
    lanes = 2 * rows * STRIDE
    tall = jnp.concatenate(
        [jnp.concatenate([x_ref[p, 0, d], x_ref[p, 1, d]], axis=0) for d in range(days)], axis=1
    )
    spread = (iota((lanes, 2 * rows), 0) // STRIDE == iota((lanes, 2 * rows), 1))
    wide = jnp.dot(spread.astype(jnp.bfloat16), tall, preferred_element_type=jnp.float32)
    keep = iota(wide.shape, 0) % STRIDE == iota(wide.shape, 1) % STRIDE
    wide = jnp.where(keep, wide, 0.0).astype(jnp.bfloat16)
    shape = (col_blocks * days, days * cols)
    row_id, lane_id = iota(shape, 0), iota(shape, 1)
    pick = (row_id // days == (lane_id % cols) // STRIDE) & (row_id % days == lane_id // cols)
    pick = jnp.where(pick, 1.0, 0.0).astype(jnp.bfloat16)
    return nt_dot(pick, wide).reshape(col_blocks, days, lanes)


def exchange_kernel(n_date, n_pol, x_ref, got_ref, blocks, send_sem, recv_sem):
    n = n_date * n_pol
    my_date, my_pol = lax.axis_index("date"), lax.axis_index("pol")
    me = my_date * n_pol + my_pol

    def place(k):
        other = lax.rem(me + k, n)
        return other // n_pol, lax.rem(other, n_pol)

    barrier = pltpu.get_barrier_semaphore()

    def greet(k, carry):
        date, pol = place(k)
        pl.semaphore_signal(
            barrier,
            inc=1,
            device_id={"date": date, "pol": pol},
            device_id_type=pl.DeviceIdType.MESH,
        )
        return carry

    lax.fori_loop(1, n, greet, 0)

    zero = jnp.zeros((1,) + blocks.shape[2:], blocks.dtype)
    for p in range(n_pol):
        blocks[p, 0:1] = zero
        blocks[p, n_date + 1 : n_date + 2] = zero
        blocks[p, 1 : n_date + 1] = pack(x_ref, p, n_date).astype(blocks.dtype)

    pl.semaphore_wait(barrier, n - 1)

    def send(k, carry):
        date, pol = place(k)
        pltpu.make_async_remote_copy(
            src_ref=blocks.at[pol, pl.ds(date, SPAN)],
            dst_ref=got_ref.at[me],
            send_sem=send_sem,
            recv_sem=recv_sem,
            device_id={"date": date, "pol": pol},
            device_id_type=pl.DeviceIdType.MESH,
        ).start()
        return carry

    lax.fori_loop(1, n, send, 0)
    pltpu.make_async_copy(
        blocks.at[my_pol, pl.ds(my_date, SPAN)], got_ref.at[me], recv_sem
    ).start()
    pltpu.make_async_copy(got_ref, got_ref, recv_sem).wait()
    sent = got_ref.at[pl.ds(0, n - 1)]
    pltpu.make_async_copy(sent, sent, send_sem).wait()


def exchange(x, n_date, n_pol):
    _, _, days, rows, _ = x.shape
    lanes = 2 * rows * STRIDE
    n = n_date * n_pol
    return pl.pallas_call(
        functools.partial(exchange_kernel, n_date, n_pol),
        out_shape=jax.ShapeDtypeStruct((n, SPAN, days, lanes), x.dtype),
        in_specs=[pl.BlockSpec(memory_space=pltpu.VMEM)],
        out_specs=pl.BlockSpec(memory_space=pltpu.VMEM),
        scratch_shapes=[
            pltpu.VMEM((n_pol, n_date + SPAN - 1, days, lanes), x.dtype),
            pltpu.SemaphoreType.DMA,
            pltpu.SemaphoreType.DMA,
        ],
        compiler_params=pltpu.CompilerParams(
            collective_id=0, has_side_effects=True, vmem_limit_bytes=24 * 1024 * 1024
        ),
    )(x)


def look_kernel(days, row_base, group_ref, refs_ref, offs_ref, got_ref, out_ref):
    sources = group_ref.shape[0]
    dates = sources * days
    if got_ref.shape[0] == SPAN:
        stored = [got_ref[m] for m in range(SPAN)]
    else:
        stored = [
            got_ref[:, m].astype(jnp.float32).reshape(dates, got_ref.shape[-1]).astype(jnp.bfloat16)
            for m in range(SPAN)
        ]
    lanes = stored[0].shape[1]
    stored = jnp.concatenate(stored, axis=1)
    width = SPAN * lanes

    slot = iota((1, dates), 1)
    held = jnp.zeros((1, dates), jnp.int32)
    for s in range(sources):
        held = jnp.where(slot // days == s, group_ref[s], held)
    held = held * days + slot % days
    ref_id = iota((NREF * REF_BLK, 1), 0)
    wanted = jnp.zeros(ref_id.shape, jnp.int32)
    for b in range(NREF):
        wanted = jnp.where(ref_id // REF_BLK == b, refs_ref[b], wanted)
    wanted = wanted * REF_BLK + ref_id % REF_BLK
    order = jnp.where(iota((dates, dates), 0) == held, 1.0, 0.0).astype(jnp.bfloat16)
    ref_order = jnp.where(wanted == held, 1.0, 0.0).astype(jnp.bfloat16)
    vals = jnp.dot(order, stored, preferred_element_type=jnp.float32)
    refs = jnp.dot(ref_order, stored, preferred_element_type=jnp.float32)

    half = lanes // 2
    turned = jnp.concatenate(
        [pltpu.roll(refs[:, m * lanes : (m + 1) * lanes], half, 1) for m in range(SPAN)], axis=1
    )
    turned = jnp.where(iota(turned.shape, 1) % lanes < half, -turned, turned)

    def window(rows, look):
        lane = iota((rows, width), 1)
        col = (lane // lanes - 1) * STRIDE + lane % STRIDE - offs_ref[1]
        row = (lane % half) // STRIDE + row_base - STRIDE * look - offs_ref[0]
        return (jnp.abs(col) <= RIM) & (jnp.abs(row) <= RIM)

    looks = out_ref.shape[1]
    square = vals * vals
    high = square.astype(jnp.bfloat16)
    low = (square - high.astype(jnp.float32)).astype(jnp.bfloat16)
    boxes = jnp.where(window(8, iota((8, width), 0)), 1.0, 0.0).astype(jnp.bfloat16)
    scale = lax.rsqrt(nt_dot(boxes, high) + nt_dot(boxes, low))

    parts, ref_scale = [], []
    for i in range(looks):
        box = jnp.where(window(1, i), 1.0, 0.0)
        here = refs * box
        parts += [here.astype(jnp.bfloat16), (turned * box).astype(jnp.bfloat16)]
        ref_scale.append(lax.rsqrt(jnp.sum(here * here, axis=1, keepdims=True)))
    num = nt_dot(jnp.concatenate(parts, axis=0), vals.astype(jnp.bfloat16))
    count = NREF * REF_BLK
    for i in range(looks):
        both = scale[i : i + 1] * ref_scale[i]
        for c in range(2):
            at = (2 * i + c) * count
            out_ref[c, i, 0] = num[at : at + count] * both


def coherences(got, date_group, ref_blocks, look_offsets, days, looks, row_base):
    dates = date_group.shape[0] * days
    smem = pl.BlockSpec(memory_space=pltpu.SMEM)
    vmem = pl.BlockSpec(memory_space=pltpu.VMEM)
    return pl.pallas_call(
        functools.partial(look_kernel, days, row_base),
        out_shape=jax.ShapeDtypeStruct((2, looks, 1, NREF * REF_BLK, dates), jnp.float32),
        in_specs=[smem, smem, smem, vmem],
        out_specs=vmem,
        compiler_params=pltpu.CompilerParams(vmem_limit_bytes=24 * 1024 * 1024),
    )(date_group, ref_blocks, look_offsets, got)


def body(slc, date_group, ref_blocks, look_offsets):
    days, rows = slc.shape[1:3]
    n_date, n_pol = lax.axis_size("date"), lax.axis_size("pol")
    looks = rows // STRIDE // n_pol
    assert slc.shape[3] == n_date * STRIDE
    if lax.axis_size("tile") == 1 and n_pol == 1:
        x, row_base = slc[None], 0
    else:
        rimmed = with_halo(slc, "tile", 2, RIM)
        step = looks * STRIDE
        x = jnp.stack([rimmed[:, :, p * step : (p + 1) * step + 2 * RIM] for p in range(n_pol)])
        row_base = -RIM
    got = exchange(x, n_date, n_pol)
    if days % 8:
        got = jnp.transpose(got, (1, 0, 2, 3)).reshape(SPAN, n_date * n_pol * days, -1)
    return coherences(got, date_group, ref_blocks, look_offsets, days, looks, row_base)


def solution(mesh):
    return jax.shard_map(
        body,
        mesh=mesh,
        in_specs=(P(None, ("date", "pol"), ("groups", "tile"), None), P(), P(), P()),
        out_specs=P(None, ("groups", "tile", "pol"), "date", None, None),
        check_vma=False,
    )
```

time: 309 us -> 13.9 us (0.04)
  waiting for transfers between devices: 149 us -> 0 us
  matrix products: 73.9 us -> 0 us
  local copies, waits for them, and re-layouts: 42.6 us -> 0.85 us
  between operations: 21.4 us -> 0.04 us
  Pallas kernels: 0 us -> 12.9 us
  other arithmetic: 12.4 us -> 0 us
  starting transfers between devices: 4.96 us -> 0 us
    psum x1 -> x0, waiting for transfers between devices: 134 us -> none  [from_root(): return lax.psum(kept, axis)]
    dot_general x74 -> x0, matrix products: 73.9 us -> none  [the longest x37 40.6 us: windowed(): jnp.einsum('...qw,cw->...qc', surface, col_box, precision=lax.Precision.H...]
    mul x64 -> x0, local copies, waits for them, and re-layouts: 22.5 us -> none  [the longest x32 11.5 us: pair_terms(): imag_one * imag_many]
    all_to_all x1 -> x0, waiting for transfers between devices: 15.1 us -> none  [body(): lax.all_to_all(arranged, ('date', 'pol'), split_axis=3, concat_axis=1, ti...]
    pallas_call x0 -> x2, Pallas kernels: none -> 12.9 us  [the longest x1 10.9 us: exchange(): pl.pallas_call(functools.partial(exchange_kernel, n_date, n_pol), out_sha...]
    while x36 -> x0, local copies, waits for them, and re-layouts: 6.71 us -> none  [the longest x4 6.59 us: body(): lax.map(one_date, (local_vals[0], local_vals[1], local_power))]
    unnamed x22 -> x8, local copies, waits for them, and re-layouts: 4.57 us -> 0.85 us
    slice x3 -> x0, local copies, waits for them, and re-layouts: 3.66 us -> none  [the longest x1 1.47 us: body(): first_date = ref_blocks[ref_block] * REF_BLK + portion_no * span_dates]
  transfers between devices with their start and end apart: 4 -> 0, of which waited for: 2 -> 0; matrix products, arithmetic and copies ran while one was open for 2% -> 0% of each run, Pallas kernels for 0% -> 0%
where the time goes in v1:
time: 13.9 us; the launch traced here: 13.8 us
  Pallas kernels  12.9 us (93%)
  local copies, waits for them, and re-layouts  0.85 us (6%)
    pallas_call x1, Pallas kernels, exchange(): pl.pallas_call(functools.partial(exchange_kernel, n_date, n_pol), out_sha...  10.9 us
    pallas_call x1, Pallas kernels, coherences(): pl.pallas_call(functools.partial(look_kernel, days, row_base), out_shape=...  2.01 us
    unnamed x8, local copies, waits for them, and re-layouts  0.85 us

profile of v1, /device:TPU:0, one launch (start us, length us, event | category | flops | bytes accessed | tf_op | source)
XLA Modules:
  0.0 13.8 jit_solution(16170160612552562433)
XLA Ops:
  0.0 0.0 copy-start
  0.0 0.8 %copy-done = bf16[2,8,16,128]{3,2,1,0:T(8,128)(2,1)S(1)} copy-done((bf16[2,8,16,128]{3,2,1,0:T(8,128)(2,1)S(1)}, bf16[2,8,16,128]{3,2,1,0:T(8,128)(2,1)}, u32[]{:S(2)}) %copy-start) | copy-done | bytes 65560
  0.8 0.0 copy-start.1
  0.8 0.0 copy-start.2
  0.8 0.0 copy-start.3
  0.8 10.9 %shard_map.46.got_ref = bf16[32,3,8,128]{3,2,1,0:T(8,128)(2,1)S(1)} custom-call(bf16[1,2,8,16,128]{4,3,2,1,0:T(8,128)(2,1)S(1)} %bitcast.1), custom_call_target="tpu_custom_call" | custom-call | tf_op jit(solution)/shard_map/pallas_call | solution.py:116
  11.7 0.0 copy-done.1
  11.7 0.0 copy-done.2
  11.7 0.0 copy-done.3
  11.7 2.0 %shard_map.47 = f32[2,4,1,64,256]{4,3,2,1,0:T(8,128)} custom-call(s32[32]{0:T(128)S(1)} %copy-done.1, s32[16]{0:T(128)S(1)} %copy-done.2, s32[4]{0:T(128)S(1)} %copy-done.3, bf16[32,3,8,128]{3,2,1,0:T(8,128)(2,1)S(1)} %shard_map.46.got_ref), custom_call_target="tpu_custom_call" | custom-call | tf_op jit(solution)/shard_map/pallas_call | solution.py:199
Async XLA Ops:
  0.0 0.8 %copy-start = (bf16[2,8,16,128]{3,2,1,0:T(8,128)(2,1)S(1)}, bf16[2,8,16,128]{3,2,1,0:T(8,128)(2,1)}, u32[]{:S(2)}) copy-start(bf16[2,8,16,128]{3,2,1,0:T(8,128)(2,1)} %param.4) | copy-start | bytes 196612
  0.8 10.9 %copy-start.1 = (s32[32]{0:T(128)S(1)}, s32[32]{0:T(128)}, u32[]{:S(2)}) copy-start(s32[32]{0:T(128)} %group_ref.1) | copy-start | bytes 388
  0.8 10.9 %copy-start.2 = (s32[16]{0:T(128)S(1)}, s32[16]{0:T(128)}, u32[]{:S(2)}) copy-start(s32[16]{0:T(128)} %refs_ref.1) | copy-start | bytes 196
  0.8 10.9 %copy-start.3 = (s32[4]{0:T(128)S(1)}, s32[4]{0:T(128)}, u32[]{:S(2)}) copy-start(s32[4]{0:T(128)} %offs_ref.1) | copy-start | bytes 52

commit v2 on v1

--- a/solution.py
+++ b/solution.py
@@ -1,4 +1,5 @@
 import functools
+import math
 
 import jax
 import jax.numpy as jnp
@@ -12,6 +13,7 @@
 STRIDE = 4
 WIN = 9
 RIM = WIN // 2
+PLANE = 8
 SPAN = 3
 
 
@@ -57,28 +59,42 @@
     return nt_dot(pick, wide).reshape(col_blocks, days, lanes)
 
 
-def exchange_kernel(n_date, n_pol, x_ref, got_ref, blocks, send_sem, recv_sem):
-    n = n_date * n_pol
+def flipped(number, bits):
+    bit = 1
+    while bit <= bits:
+        if bits & bit:
+            number = number + bit - 2 * bit * lax.rem(number // bit, 2)
+        bit *= 2
+    return number
+
+
+def exchange_kernel(
+    n_plane, side, n_pol, x_ref, got_ref, blocks, stage, send_one, recv_one, send_two, recv_two
+):
+    n_date, first = n_plane * side, n_plane * n_pol
     my_date, my_pol = lax.axis_index("date"), lax.axis_index("pol")
-    me = my_date * n_pol + my_pol
-
-    def place(k):
-        other = lax.rem(me + k, n)
-        return other // n_pol, lax.rem(other, n_pol)
+    my_plane, my_place = my_date // side, lax.rem(my_date, side)
+    me = my_plane * n_pol + my_pol
+
+    def across(t):
+        other = flipped(me, t)
+        plane, pol = other // n_pol, lax.rem(other, n_pol)
+        return other, plane, pol, {"date": plane * side + my_place, "pol": pol}
+
+    def beside(k):
+        place = lax.rem(my_place + k, side)
+        return place, {"date": my_plane * side + place, "pol": my_pol}
 
     barrier = pltpu.get_barrier_semaphore()
+    mesh_ids = pl.DeviceIdType.MESH
 
     def greet(k, carry):
-        date, pol = place(k)
-        pl.semaphore_signal(
-            barrier,
-            inc=1,
-            device_id={"date": date, "pol": pol},
-            device_id_type=pl.DeviceIdType.MESH,
-        )
+        pl.semaphore_signal(barrier, inc=1, device_id=beside(k)[1], device_id_type=mesh_ids)
         return carry
 
-    lax.fori_loop(1, n, greet, 0)
+    for t in range(first - 1, 0, -1):
+        pl.semaphore_signal(barrier, inc=1, device_id=across(t)[3], device_id_type=mesh_ids)
+    lax.fori_loop(1, side, greet, 0)
 
     zero = jnp.zeros((1,) + blocks.shape[2:], blocks.dtype)
     for p in range(n_pol):
@@ -86,40 +102,67 @@
         blocks[p, n_date + 1 : n_date + 2] = zero
         blocks[p, 1 : n_date + 1] = pack(x_ref, p, n_date).astype(blocks.dtype)
 
-    pl.semaphore_wait(barrier, n - 1)
-
-    def send(k, carry):
-        date, pol = place(k)
+    pl.semaphore_wait(barrier, first + side - 2)
+
+    reach = side + SPAN - 1
+    for t in range(first - 1, 0, -1):
+        _, plane, pol, device = across(t)
         pltpu.make_async_remote_copy(
-            src_ref=blocks.at[pol, pl.ds(date, SPAN)],
-            dst_ref=got_ref.at[me],
-            send_sem=send_sem,
-            recv_sem=recv_sem,
-            device_id={"date": date, "pol": pol},
-            device_id_type=pl.DeviceIdType.MESH,
+            src_ref=blocks.at[pol, pl.ds(plane * side, reach)],
+            dst_ref=stage.at[me],
+            send_sem=send_one,
+            recv_sem=recv_one.at[me],
+            device_id=device,
+            device_id_type=mesh_ids,
         ).start()
-        return carry
-
-    lax.fori_loop(1, n, send, 0)
-    pltpu.make_async_copy(
-        blocks.at[my_pol, pl.ds(my_date, SPAN)], got_ref.at[me], recv_sem
-    ).start()
-    pltpu.make_async_copy(got_ref, got_ref, recv_sem).wait()
-    sent = got_ref.at[pl.ds(0, n - 1)]
-    pltpu.make_async_copy(sent, sent, send_sem).wait()
+
+    def share(origin, source, start):
+        def give(k, carry):
+            place, device = beside(k)
+            pltpu.make_async_remote_copy(
+                src_ref=source.at[pl.ds(start + place, SPAN)],
+                dst_ref=got_ref.at[origin, my_place],
+                send_sem=send_two,
+                recv_sem=recv_two,
+                device_id=device,
+                device_id_type=mesh_ids,
+            ).start()
+            return carry
+
+        lax.fori_loop(1, side, give, 0)
+        pltpu.make_async_copy(
+            source.at[pl.ds(start + my_place, SPAN)], got_ref.at[origin, my_place], recv_two
+        ).start()
+
+    share(me, blocks.at[my_pol], my_plane * side)
+    for t in range(1, first):
+        other = across(t)[0]
+        pltpu.make_async_copy(stage.at[other], stage.at[other], recv_one.at[other]).wait()
+        share(other, stage.at[other], 0)
+
+    pltpu.make_async_copy(got_ref, got_ref, recv_two).wait()
+    sent = stage.at[pl.ds(0, first - 1)]
+    pltpu.make_async_copy(sent, sent, send_one).wait()
+    sent = got_ref.at[:, pl.ds(0, side - 1)]
+    pltpu.make_async_copy(sent, sent, send_two).wait()
 
 
 def exchange(x, n_date, n_pol):
     _, _, days, rows, _ = x.shape
     lanes = 2 * rows * STRIDE
-    n = n_date * n_pol
-    return pl.pallas_call(
-        functools.partial(exchange_kernel, n_date, n_pol),
-        out_shape=jax.ShapeDtypeStruct((n, SPAN, days, lanes), x.dtype),
+    side = math.gcd(n_date, PLANE)
+    n_plane = n_date // side
+    first = n_plane * n_pol
+    got = pl.pallas_call(
+        functools.partial(exchange_kernel, n_plane, side, n_pol),
+        out_shape=jax.ShapeDtypeStruct((first, side, SPAN, days, lanes), x.dtype),
         in_specs=[pl.BlockSpec(memory_space=pltpu.VMEM)],
         out_specs=pl.BlockSpec(memory_space=pltpu.VMEM),
         scratch_shapes=[
             pltpu.VMEM((n_pol, n_date + SPAN - 1, days, lanes), x.dtype),
+            pltpu.VMEM((first, side + SPAN - 1, days, lanes), x.dtype),
+            pltpu.SemaphoreType.DMA,
+            pltpu.SemaphoreType.DMA((first,)),
             pltpu.SemaphoreType.DMA,
             pltpu.SemaphoreType.DMA,
         ],
@@ -127,6 +170,10 @@
             collective_id=0, has_side_effects=True, vmem_limit_bytes=24 * 1024 * 1024
         ),
     )(x)
+    if n_pol > 1:
+        got = got.reshape(n_plane, n_pol, side, SPAN, days, lanes)
+        got = jnp.swapaxes(got, 1, 2)
+    return got.reshape(n_date * n_pol, SPAN, days, lanes)
 
 
 def look_kernel(days, row_base, group_ref, refs_ref, offs_ref, got_ref, out_ref):

time: 13.9 us -> 16.1 us (1.16)
  Pallas kernels: 12.9 us -> 14.4 us
  local copies, waits for them, and re-layouts: 0.85 us -> 1.5 us
    pallas_call x1, Pallas kernels: 10.9 us -> 12.4 us  [exchange(): pl.pallas_call(functools.partial(exchange_kernel, n_plane, side, n_pol),...]
    unnamed x8, local copies, waits for them, and re-layouts: 0.85 us -> 1.5 us
where the time goes in v2:
time: 16.1 us; the launch traced here: 15.9 us
  Pallas kernels  14.4 us (89%)
  local copies, waits for them, and re-layouts  1.5 us (9%)
    pallas_call x1, Pallas kernels, exchange(): pl.pallas_call(functools.partial(exchange_kernel, n_plane, side, n_pol),...  12.4 us
    pallas_call x1, Pallas kernels, coherences(): pl.pallas_call(functools.partial(look_kernel, days, row_base), out_shape=...  2.02 us
    unnamed x8, local copies, waits for them, and re-layouts  1.5 us

profile of v2, /device:TPU:0, one launch (start us, length us, event | category | flops | bytes accessed | tf_op | source)
XLA Modules:
  0.0 15.9 jit_solution(9577193242451870336)
XLA Ops:
  0.0 0.0 copy-start
  0.0 0.8 %copy-done = bf16[2,8,16,128]{3,2,1,0:T(8,128)(2,1)S(1)} copy-done((bf16[2,8,16,128]{3,2,1,0:T(8,128)(2,1)S(1)}, bf16[2,8,16,128]{3,2,1,0:T(8,128)(2,1)}, u32[]{:S(2)}) %copy-start) | copy-done | bytes 65560
  0.8 12.4 %shard_map.46 = bf16[4,8,3,8,128]{4,3,2,1,0:T(8,128)(2,1)S(1)} custom-call(bf16[1,2,8,16,128]{4,3,2,1,0:T(8,128)(2,1)S(1)} %bitcast.3), custom_call_target="tpu_custom_call" | custom-call | tf_op jit(solution)/shard_map/pallas_call | solution.py:156
  13.2 0.0 copy-start.1
  13.2 0.0 copy-start.2
  13.3 0.0 copy-start.3
  13.3 0.6 %copy-done.1 = s32[32]{0:T(128)S(1)} copy-done((s32[32]{0:T(128)S(1)}, s32[32]{0:T(128)}, u32[]{:S(2)}) %copy-start.1) | copy-done | bytes 152
  13.9 0.0 copy-done.2
  13.9 0.0 copy-done.3
  13.9 2.0 %shard_map.47 = f32[2,4,1,64,256]{4,3,2,1,0:T(8,128)} custom-call(s32[32]{0:T(128)S(1)} %copy-done.1, s32[16]{0:T(128)S(1)} %copy-done.2, s32[4]{0:T(128)S(1)} %copy-done.3, bf16[32,3,8,128]{3,2,1,0:T(8,128)(2,1)S(1)} %bitcast.2), custom_call_target="tpu_custom_call" | custom-call | tf_op jit(solution)/shard_map/pallas_call | solution.py:246
Async XLA Ops:
  0.0 0.8 %copy-start = (bf16[2,8,16,128]{3,2,1,0:T(8,128)(2,1)S(1)}, bf16[2,8,16,128]{3,2,1,0:T(8,128)(2,1)}, u32[]{:S(2)}) copy-start(bf16[2,8,16,128]{3,2,1,0:T(8,128)(2,1)} %param.4) | copy-start | bytes 196612
  13.2 0.7 %copy-start.1 = (s32[32]{0:T(128)S(1)}, s32[32]{0:T(128)}, u32[]{:S(2)}) copy-start(s32[32]{0:T(128)} %group_ref.1) | copy-start | bytes 388
  13.2 0.7 %copy-start.2 = (s32[16]{0:T(128)S(1)}, s32[16]{0:T(128)}, u32[]{:S(2)}) copy-start(s32[16]{0:T(128)} %refs_ref.1) | copy-start | bytes 196
  13.3 0.7 %copy-start.3 = (s32[4]{0:T(128)S(1)}, s32[4]{0:T(128)}, u32[]{:S(2)}) copy-start(s32[4]{0:T(128)} %offs_ref.1) | copy-start | bytes 52

commit v3 on v1

--- a/solution.py
+++ b/solution.py
@@ -40,19 +40,32 @@
     return lax.broadcasted_iota(jnp.int32, shape, dim)
 
 
+def over(ids, size):
+    if size & (size - 1):
+        return ids // size
+    return ids >> (size.bit_length() - 1)
+
+
+def within(ids, size):
+    if size & (size - 1):
+        return ids % size
+    return ids & (size - 1)
+
+
 def pack(x_ref, p, col_blocks):
     _, _, days, rows, cols = x_ref.shape
     lanes = 2 * rows * STRIDE
     tall = jnp.concatenate(
         [jnp.concatenate([x_ref[p, 0, d], x_ref[p, 1, d]], axis=0) for d in range(days)], axis=1
     )
-    spread = (iota((lanes, 2 * rows), 0) // STRIDE == iota((lanes, 2 * rows), 1))
-    wide = jnp.dot(spread.astype(jnp.bfloat16), tall, preferred_element_type=jnp.float32)
-    keep = iota(wide.shape, 0) % STRIDE == iota(wide.shape, 1) % STRIDE
+    spread = over(iota((lanes, 2 * rows), 0), STRIDE) == iota((lanes, 2 * rows), 1)
+    spread = jnp.where(spread, 1.0, 0.0).astype(jnp.bfloat16)
+    wide = jnp.dot(spread, tall, preferred_element_type=jnp.float32)
+    lane = iota((1, days * cols), 1)
+    keep = within(iota((lanes, 1), 0), STRIDE) == within(lane, STRIDE)
     wide = jnp.where(keep, wide, 0.0).astype(jnp.bfloat16)
-    shape = (col_blocks * days, days * cols)
-    row_id, lane_id = iota(shape, 0), iota(shape, 1)
-    pick = (row_id // days == (lane_id % cols) // STRIDE) & (row_id % days == lane_id // cols)
+    target = over(within(lane, cols), STRIDE) * days + over(lane, cols)
+    pick = iota((col_blocks * days, days * cols), 0) == target
     pick = jnp.where(pick, 1.0, 0.0).astype(jnp.bfloat16)
     return nt_dot(pick, wide).reshape(col_blocks, days, lanes)
 
@@ -64,6 +77,8 @@
 
     def place(k):
         other = lax.rem(me + k, n)
+        if n_pol == 1:
+            return other, 0
         return other // n_pol, lax.rem(other, n_pol)
 
     barrier = pltpu.get_barrier_semaphore()
@@ -145,14 +160,15 @@
 
     slot = iota((1, dates), 1)
     held = jnp.zeros((1, dates), jnp.int32)
+    block = over(slot, days)
     for s in range(sources):
-        held = jnp.where(slot // days == s, group_ref[s], held)
-    held = held * days + slot % days
+        held = jnp.where(block == s, group_ref[s], held)
+    held = held * days + within(slot, days)
     ref_id = iota((NREF * REF_BLK, 1), 0)
     wanted = jnp.zeros(ref_id.shape, jnp.int32)
     for b in range(NREF):
-        wanted = jnp.where(ref_id // REF_BLK == b, refs_ref[b], wanted)
-    wanted = wanted * REF_BLK + ref_id % REF_BLK
+        wanted = jnp.where(over(ref_id, REF_BLK) == b, refs_ref[b], wanted)
+    wanted = wanted * REF_BLK + within(ref_id, REF_BLK)
     order = jnp.where(iota((dates, dates), 0) == held, 1.0, 0.0).astype(jnp.bfloat16)
     ref_order = jnp.where(wanted == held, 1.0, 0.0).astype(jnp.bfloat16)
     vals = jnp.dot(order, stored, preferred_element_type=jnp.float32)
@@ -162,12 +178,13 @@
     turned = jnp.concatenate(
         [pltpu.roll(refs[:, m * lanes : (m + 1) * lanes], half, 1) for m in range(SPAN)], axis=1
     )
-    turned = jnp.where(iota(turned.shape, 1) % lanes < half, -turned, turned)
+    sign = jnp.where(within(iota((1, width), 1), lanes) < half, -1.0, 1.0)
+    turned = turned * sign
 
     def window(rows, look):
         lane = iota((rows, width), 1)
-        col = (lane // lanes - 1) * STRIDE + lane % STRIDE - offs_ref[1]
-        row = (lane % half) // STRIDE + row_base - STRIDE * look - offs_ref[0]
+        col = (over(lane, lanes) - 1) * STRIDE + within(lane, STRIDE) - offs_ref[1]
+        row = over(within(lane, half), STRIDE) + row_base - STRIDE * look - offs_ref[0]
         return (jnp.abs(col) <= RIM) & (jnp.abs(row) <= RIM)
 
     looks = out_ref.shape[1]

time: 13.9 us -> 13.9 us (level)
  no operation moved by 1% of the time
where the time goes in v3:
time: 13.9 us; the launch traced here: 13.8 us
  Pallas kernels  12.9 us (93%)
  local copies, waits for them, and re-layouts  0.85 us (6%)
    pallas_call x1, Pallas kernels, exchange(): pl.pallas_call(functools.partial(exchange_kernel, n_date, n_pol), out_sha...  10.9 us
    pallas_call x1, Pallas kernels, coherences(): pl.pallas_call(functools.partial(look_kernel, days, row_base), out_shape=...  2.02 us
    unnamed x8, local copies, waits for them, and re-layouts  0.85 us

profile of v3, /device:TPU:0, one launch (start us, length us, event | category | flops | bytes accessed | tf_op | source)
XLA Modules:
  0.0 13.8 jit_solution(12555662773372250972)
XLA Ops:
  0.0 0.0 copy-start
  0.0 0.8 %copy-done = bf16[2,8,16,128]{3,2,1,0:T(8,128)(2,1)S(1)} copy-done((bf16[2,8,16,128]{3,2,1,0:T(8,128)(2,1)S(1)}, bf16[2,8,16,128]{3,2,1,0:T(8,128)(2,1)}, u32[]{:S(2)}) %copy-start) | copy-done | bytes 65560
  0.8 0.0 copy-start.1
  0.8 0.0 copy-start.2
  0.8 0.0 copy-start.3
  0.8 10.9 %shard_map.46.got_ref = bf16[32,3,8,128]{3,2,1,0:T(8,128)(2,1)S(1)} custom-call(bf16[1,2,8,16,128]{4,3,2,1,0:T(8,128)(2,1)S(1)} %bitcast.1), custom_call_target="tpu_custom_call" | custom-call | tf_op jit(solution)/shard_map/pallas_call | solution.py:131
  11.7 0.0 copy-done.1
  11.7 0.0 copy-done.2
  11.7 0.0 copy-done.3
  11.7 2.0 %shard_map.47 = f32[2,4,1,64,256]{4,3,2,1,0:T(8,128)} custom-call(s32[32]{0:T(128)S(1)} %copy-done.1, s32[16]{0:T(128)S(1)} %copy-done.2, s32[4]{0:T(128)S(1)} %copy-done.3, bf16[32,3,8,128]{3,2,1,0:T(8,128)(2,1)S(1)} %shard_map.46.got_ref), custom_call_target="tpu_custom_call" | custom-call | tf_op jit(solution)/shard_map/pallas_call | solution.py:216
Async XLA Ops:
  0.0 0.8 %copy-start = (bf16[2,8,16,128]{3,2,1,0:T(8,128)(2,1)S(1)}, bf16[2,8,16,128]{3,2,1,0:T(8,128)(2,1)}, u32[]{:S(2)}) copy-start(bf16[2,8,16,128]{3,2,1,0:T(8,128)(2,1)} %param.4) | copy-start | bytes 196612
  0.8 10.9 %copy-start.1 = (s32[32]{0:T(128)S(1)}, s32[32]{0:T(128)}, u32[]{:S(2)}) copy-start(s32[32]{0:T(128)} %group_ref.1) | copy-start | bytes 388
  0.8 10.9 %copy-start.2 = (s32[16]{0:T(128)S(1)}, s32[16]{0:T(128)}, u32[]{:S(2)}) copy-start(s32[16]{0:T(128)} %refs_ref.1) | copy-start | bytes 196
  0.8 10.9 %copy-start.3 = (s32[4]{0:T(128)S(1)}, s32[4]{0:T(128)}, u32[]{:S(2)}) copy-start(s32[4]{0:T(128)} %offs_ref.1) | copy-start | bytes 52

commit v4 on v3

--- a/solution.py
+++ b/solution.py
@@ -103,8 +103,8 @@
 
     pl.semaphore_wait(barrier, n - 1)
 
-    def send(k, carry):
-        date, pol = place(k)
+    def send(step, carry):
+        date, pol = place(n // 2 + (step // 2) * (2 * lax.rem(step, 2) - 1))
         pltpu.make_async_remote_copy(
             src_ref=blocks.at[pol, pl.ds(date, SPAN)],
             dst_ref=got_ref.at[me],

time: 13.9 us -> 15.6 us (1.12)
  Pallas kernels: 12.9 us -> 14.5 us
    pallas_call x1, Pallas kernels: 10.9 us -> 12.5 us  [exchange(): pl.pallas_call(functools.partial(exchange_kernel, n_date, n_pol), out_sha...]
where the time goes in v4:
time: 15.6 us; the launch traced here: 15.4 us
  Pallas kernels  14.5 us (93%)
  local copies, waits for them, and re-layouts  0.85 us (5%)
    pallas_call x1, Pallas kernels, exchange(): pl.pallas_call(functools.partial(exchange_kernel, n_date, n_pol), out_sha...  12.5 us
    pallas_call x1, Pallas kernels, coherences(): pl.pallas_call(functools.partial(look_kernel, days, row_base), out_shape=...  2.02 us
    unnamed x8, local copies, waits for them, and re-layouts  0.85 us

profile of v4, /device:TPU:0, one launch (start us, length us, event | category | flops | bytes accessed | tf_op | source)
XLA Modules:
  0.0 15.4 jit_solution(3990787839860263036)
XLA Ops:
  0.0 0.0 copy-start
  0.0 0.8 %copy-done = bf16[2,8,16,128]{3,2,1,0:T(8,128)(2,1)S(1)} copy-done((bf16[2,8,16,128]{3,2,1,0:T(8,128)(2,1)S(1)}, bf16[2,8,16,128]{3,2,1,0:T(8,128)(2,1)}, u32[]{:S(2)}) %copy-start) | copy-done | bytes 65560
  0.8 0.0 copy-start.1
  0.8 0.0 copy-start.2
  0.8 0.0 copy-start.3
  0.8 12.5 %shard_map.46.got_ref = bf16[32,3,8,128]{3,2,1,0:T(8,128)(2,1)S(1)} custom-call(bf16[1,2,8,16,128]{4,3,2,1,0:T(8,128)(2,1)S(1)} %bitcast.1), custom_call_target="tpu_custom_call" | custom-call | tf_op jit(solution)/shard_map/pallas_call | solution.py:131
  13.4 0.0 copy-done.1
  13.4 0.0 copy-done.2
  13.4 0.0 copy-done.3
  13.4 2.0 %shard_map.47 = f32[2,4,1,64,256]{4,3,2,1,0:T(8,128)} custom-call(s32[32]{0:T(128)S(1)} %copy-done.1, s32[16]{0:T(128)S(1)} %copy-done.2, s32[4]{0:T(128)S(1)} %copy-done.3, bf16[32,3,8,128]{3,2,1,0:T(8,128)(2,1)S(1)} %shard_map.46.got_ref), custom_call_target="tpu_custom_call" | custom-call | tf_op jit(solution)/shard_map/pallas_call | solution.py:216
Async XLA Ops:
  0.0 0.8 %copy-start = (bf16[2,8,16,128]{3,2,1,0:T(8,128)(2,1)S(1)}, bf16[2,8,16,128]{3,2,1,0:T(8,128)(2,1)}, u32[]{:S(2)}) copy-start(bf16[2,8,16,128]{3,2,1,0:T(8,128)(2,1)} %param.4) | copy-start | bytes 196612
  0.8 12.5 %copy-start.1 = (s32[32]{0:T(128)S(1)}, s32[32]{0:T(128)}, u32[]{:S(2)}) copy-start(s32[32]{0:T(128)} %group_ref.1) | copy-start | bytes 388
  0.8 12.5 %copy-start.2 = (s32[16]{0:T(128)S(1)}, s32[16]{0:T(128)}, u32[]{:S(2)}) copy-start(s32[16]{0:T(128)} %refs_ref.1) | copy-start | bytes 196
  0.8 12.5 %copy-start.3 = (s32[4]{0:T(128)S(1)}, s32[4]{0:T(128)}, u32[]{:S(2)}) copy-start(s32[4]{0:T(128)} %offs_ref.1) | copy-start | bytes 52
